TPU v7x, 512 devices: a whole 4x8x8 slice. The times are simulated.
512 devices in a mesh: ctx: 32 (over z, y_hi, core), tp: 16 (over x, y_lo).
Axes of the slice: x: 4, y: 8 (y_hi: 2, y_lo: 4; y = y_hi * 4 + y_lo), z: 8, core: 2. Of those that a mesh axis runs over, the one named last changes fastest.
Arguments:
- queries: bfloat16 [4096, 32, 128], P('ctx', 'tp'), may hold values from -6 to 6
- incoming_keys: bfloat16 [4096, 4, 128], P('ctx'), may hold values from -6 to 6
- incoming_values: bfloat16 [4096, 4, 128], P('ctx'), may hold values from -6 to 6
- cache_keys: bfloat16 [8192, 4, 128], P('ctx'), may hold values from -6 to 6
- stored_value_rows: bfloat16 [8192, 4, 128], P('ctx'), may hold values from -6 to 6
- cache_valid: int32 [32], P('ctx'), may hold values from 1 to 256, 4096 in all
- out_weight: bfloat16 [4096, 8192], P('tp'), may hold values from -3 to 3
Outputs:
- projected: bfloat16 [4096, 8192], P('ctx', 'tp')
Inputs may be any that keep to these rules, and one draw needn't show every extreme that they name: `cache_valid`: each cache block has at least one live slot.
All inputs are finite; a program needn't handle non-finite values.
Results may differ from a plain program's by a relative error of at most 0.024.
Values may be sent and summed in bfloat16 or wider, within the bound.
A program may use at most 64 MiB of HBM per device.

v0:
```python
import jax
import jax.numpy as jnp
from jax import lax
from jax.sharding import PartitionSpec as P

QUERY_HEADS = 32
KEY_VALUE_HEADS = 4


masked_score = -1e30
far_position = 2**30


def absorb(running, key_block, value_block, key_pos, query_rows, query_pos):
    row_max, row_sum, weighted = running
    scale_factor = query_rows.shape[1] ** (-0.5)
    scores = (
        lax.dot_general(
            query_rows, key_block, (((1,), (1,)), ((), ())), preferred_element_type=jnp.float32
        )
        * scale_factor
    )
    scores = jnp.where(key_pos[None, :] <= query_pos[:, None], scores, masked_score)
    new_max = jnp.maximum(row_max, jnp.max(scores, axis=1))
    rescale = jnp.exp(row_max - new_max)
    weights = jnp.exp(scores - new_max[:, None])
    new_sum = row_sum * rescale + jnp.sum(weights, axis=1)
    new_weighted = weighted * rescale[:, None] + jnp.dot(
        weights.astype(jnp.bfloat16), value_block, preferred_element_type=jnp.float32
    )
    return (new_max, new_sum, new_weighted)


def local(
    queries, incoming_keys, incoming_values, cache_keys, stored_value_rows, cache_valid, out_weight
):
    tok_rows = queries.shape[0]
    local_heads = queries.shape[1]
    head_size = queries.shape[2]
    row_count = tok_rows * local_heads
    query_rows = queries.reshape(row_count, head_size)
    first_pos = lax.axis_index("ctx") * tok_rows
    query_pos = first_pos + jnp.arange(row_count, dtype=jnp.int32) // local_heads
    last_pos = first_pos + tok_rows - 1
    key_value_head = lax.axis_index("tp") * local_heads // (QUERY_HEADS // KEY_VALUE_HEADS)
    cache_key = lax.dynamic_index_in_dim(cache_keys, key_value_head, 1, keepdims=False)
    cache_value = lax.dynamic_index_in_dim(stored_value_rows, key_value_head, 1, keepdims=False)
    fresh_key = lax.dynamic_index_in_dim(incoming_keys, key_value_head, 1, keepdims=False)
    fresh_value = lax.dynamic_index_in_dim(incoming_values, key_value_head, 1, keepdims=False)
    cache_len = cache_keys.shape[0]
    cache_pos = jnp.where(
        jnp.arange(cache_len, dtype=jnp.int32) < cache_valid[0], -1, far_position
    ).astype(jnp.int32)
    start_state = (
        jnp.full((row_count,), masked_score, jnp.float32),
        jnp.zeros((row_count,), jnp.float32),
        jnp.zeros((row_count, head_size), jnp.float32),
    )
    key_block = lax.all_gather(cache_key, "ctx", axis=0, tiled=True)
    value_block = lax.all_gather(cache_value, "ctx", axis=0, tiled=True)
    key_pos = lax.all_gather(cache_pos, "ctx", axis=0, tiled=True)
    running = absorb(start_state, key_block, value_block, key_pos, query_rows, query_pos)
    key_block = lax.all_gather(fresh_key, "ctx", axis=0, tiled=True)
    value_block = lax.all_gather(fresh_value, "ctx", axis=0, tiled=True)
    key_pos = jnp.arange(key_block.shape[0], dtype=jnp.int32)
    running = lax.cond(
        jnp.int32(0) <= last_pos,
        lambda state: absorb(state, key_block, value_block, key_pos, query_rows, query_pos),
        lambda state: state,
        running,
    )
    row_max, row_sum, weighted = running
    attended = (
        (weighted / row_sum[:, None])
        .astype(jnp.bfloat16)
        .reshape(tok_rows, local_heads * head_size)
    )
    partial_term = jnp.dot(attended, out_weight, preferred_element_type=jnp.float32)
    summed = lax.psum_scatter(
        partial_term.astype(jnp.bfloat16), "tp", scatter_dimension=1, tiled=True
    )
    return summed


def solution(mesh):
    placed = (
        P("ctx", "tp", None),
        P("ctx", None, None),
        P("ctx", None, None),
        P("ctx", None, None),
        P("ctx", None, None),
        P("ctx"),
        P("tp", None),
    )
    return jax.shard_map(
        local, mesh=mesh, in_specs=placed, out_specs=P("ctx", "tp"), check_vma=False
    )
```

profile of v0, /device:TPU:64, one launch (start us, length us, event | category | flops | bytes accessed | tf_op | source)
XLA Modules:
  0.0 471.7 jit_solution(15832802909263082329)
XLA Ops:
  6.5 0.9 copy-done
  7.5 0.1 constant_dynamic-slice_fusion.3
  7.6 0.6 copy.18
  8.3 0.0 all-gather.10.cloned.1.call-update
  8.3 0.0 all-gather.12.cloned.1.call-start
  8.3 1.1 constant_dynamic-slice_fusion.2
  9.4 0.6 copy.19
  10.1 0.0 all-gather.12.cloned.1.call-update
  10.1 0.0 all-gather.14.cloned.1.call-start
  10.1 1.0 constant_dynamic-slice_fusion.1
  11.1 0.6 copy.20
  11.8 0.0 all-gather.16.cloned.1.call-start
  11.8 1.0 constant_dynamic-slice_fusion
  12.8 0.6 copy.21
  13.4 0.0 reduce-scatter.2.cloned.1.call-start
  14.2 57.3 %all-gather.4 = s32[32,1,256]{2,1,0:T(1,128)S(1)} all-gather(s32[1,1,256]{2,1,0:T(1,128)S(1)} %bitcast.29), channel_id=1, replica_groups=mesh['ctx'=32,'tp'=16] {'ctx'}, dimensions={0}, use_global_device_ids=true | all-gather | bytes 33792 | tf_op jit(solution)/shard_map/all_gather | solution.py:61
  71.5 33.6 %all-gather.10.cloned.1.call-done = bf16[8192,1,128]{2,0,1:T(8,128)(2,1)} async-done(((bf16[256,1,128]{2,0,1:T(8,128)(2,1)}), bf16[8192,1,128]{2,0,1:T(8,128)(2,1)}) %all-gather.10.cloned.1.call-update) | async-done | bytes 2097168 | tf_op jit(solution)/shard_map/all_gather | solution.py:59
  105.1 5.6 %fusion.27 = (f32[256]{0:T(256)S(1)}, f32[256,8192]{0,1:T(8,128)S(1)}) fusion(bf16[256,128]{1,0:T(8,128)(2,1)} %bitcast.31, bf16[8192,1,128]{2,0,1:T(8,128)(2,1)} %all-gather.10.cloned.1.call-done, s32[256]{0:T(256)S(1)} %fusion.24, s32[8192]{0:T(1024)S(1)} %bitcast.28), kind=kOutput, calls=%fused_computation.39 | convolution fusion | flops 545259264 | bytes 10586112 | tf_op jit(solution)/shard_map/dot_general | solution.py:18
  110.8 1.2 fusion.13
  112.0 2.0 copy-done.1
  114.0 81.7 %all-gather.12.cloned.1.call-done = bf16[8192,1,128]{2,0,1:T(8,128)(2,1)} async-done(((bf16[256,1,128]{2,0,1:T(8,128)(2,1)}), bf16[8192,1,128]{2,0,1:T(8,128)(2,1)}) %all-gather.12.cloned.1.call-update) | async-done | bytes 2097168 | tf_op jit(solution)/shard_map/all_gather | solution.py:60
  195.7 5.6 %fusion.19 = f32[256,128]{1,0:T(8,128)S(1)} fusion(bf16[8192,1,128]{2,0,1:T(8,128)(2,1)} %all-gather.12.cloned.1.call-done, f32[256,8192]{0,1:T(8,128)} %copy-done.1, f32[256]{0:T(256)S(1)} %broadcast_maximum_fusion, f32[256]{0:T(256)S(1)} %get-tuple-element.98), kind=kOutput, calls=%fused_computation.23 | convolution fusion | flops 541097984 | bytes 10618880 | tf_op jit(solution)/shard_map/dot_general | solution.py:28
  201.3 79.3 %all-gather.14.cloned.1.call-done = bf16[4096,1,128]{2,0,1:T(8,128)(2,1)} async-done(((bf16[128,1,128]{2,0,1:T(8,128)(2,1)}), bf16[4096,1,128]{2,0,1:T(8,128)(2,1)}) %all-gather.14.cloned.1.call-update) | async-done | bytes 1048592 | tf_op jit(solution)/shard_map/all_gather | solution.py:63
  280.7 84.7 %all-gather.16.cloned.1.call-done = bf16[4096,1,128]{2,0,1:T(8,128)(2,1)} async-done(((bf16[128,1,128]{2,0,1:T(8,128)(2,1)}), bf16[4096,1,128]{2,0,1:T(8,128)(2,1)}) %all-gather.16.cloned.1.call-update) | async-done | bytes 1048592 | tf_op jit(solution)/shard_map/all_gather | solution.py:64
  365.4 3.9 conditional.1
  365.5 2.2 fusion.26
  367.7 0.7 fusion.2
  368.4 0.9 fusion.6
  369.3 0.1 divide_convert_fusion
  369.4 4.2 convolution_convert_fusion
  373.7 0.0 reduce-scatter.2.cloned.1.call-update
  373.7 91.5 %reduce-scatter.2.cloned.1.call-done = bf16[128,512]{1,0:T(8,128)(2,1)} async-done(((bf16[128,8192]{1,0:T(8,128)(2,1)}), bf16[128,512]{1,0:T(8,128)(2,1)}) %reduce-scatter.2.cloned.1.call-update) | async-done | bytes 131088 | tf_op jit(solution)/shard_map/reduce_scatter | solution.py:79
  (22 shorter events, 0.1 us)
Async XLA Ops:
  6.5 1.0 copy-start
  6.5 98.6 %all-gather.10.cloned.1.call-start = ((), (), s32[]{:S(2)}) async-start(), calls=%async_computation.2 | async-start | bytes 2162688 | tf_op jit(solution)/shard_map/all_gather | solution.py:59
  8.3 187.4 %all-gather.12.cloned.1.call-start = ((), (), s32[]{:S(2)}) async-start(), calls=%async_computation.3 | async-start | bytes 2162688 | tf_op jit(solution)/shard_map/all_gather | solution.py:60
  10.1 270.6 %all-gather.14.cloned.1.call-start = ((), (), s32[]{:S(2)}) async-start(), calls=%async_computation.4 | async-start | bytes 1081344 | tf_op jit(solution)/shard_map/all_gather | solution.py:63
  11.8 353.6 %all-gather.16.cloned.1.call-start = ((), (), s32[]{:S(2)}) async-start(), calls=%async_computation.5 | async-start | bytes 1081344 | tf_op jit(solution)/shard_map/all_gather | solution.py:64
  13.4 451.7 %reduce-scatter.2.cloned.1.call-start = ((), (), s32[]{:S(2)}) async-start(), calls=%async_computation.1 | async-start | bytes 2228224 | tf_op jit(solution)/shard_map/reduce_scatter | solution.py:79
  110.8 3.2 copy-start.1
  195.7 169.7 %copy-start.3 = (bf16[128,2,128]{2,1,0:T(2,128)(2,1)S(1)}, bf16[128,2,128]{2,1,0:T(2,128)(2,1)}, u32[]{:S(2)}) copy-start(bf16[128,2,128]{2,1,0:T(2,128)(2,1)} %param.9) | copy-start | bytes 196612
  365.4 3.0 copy-start.2
Sparse Core Ops, SparseCore 0:
  10.7 94.3 all-gather.9
  108.5 87.1 all-gather.11
  199.1 81.5 all-gather.13
  283.9 81.4 all-gather.15
  373.8 91.2 reduce-scatter.1
where the time goes:
time: 472 us
  waiting for transfers between devices  371 us (79%)
  blocking collectives  57.3 us (12%)
  matrix products  18.6 us (4%)
  between operations  13.9 us (3%)
  local copies, waits for them, and re-layouts  8.71 us (2%)
    reduce_scatter x1, waiting for transfers between devices, local(): lax.psum_scatter(partial_term.astype(jnp.bfloat16), 'tp', scatter_dimensi...  91.5 us
    all_gather x1, waiting for transfers between devices, local(): value_block = lax.all_gather(fresh_value, 'ctx', axis=0, tiled=True)  84.7 us
    all_gather x1, waiting for transfers between devices, local(): value_block = lax.all_gather(cache_value, 'ctx', axis=0, tiled=True)  81.7 us
    all_gather x1, waiting for transfers between devices, local(): key_block = lax.all_gather(fresh_key, 'ctx', axis=0, tiled=True)  79.3 us
    all_gather x1, blocking collectives, local(): key_pos = lax.all_gather(cache_pos, 'ctx', axis=0, tiled=True)  57.3 us
    all_gather x1, waiting for transfers between devices, local(): key_block = lax.all_gather(cache_key, 'ctx', axis=0, tiled=True)  33.6 us
  transfers between devices with their start and end apart: 5, of which 5 were waited for; matrix products, arithmetic and copies ran while one was open for 4% of the time, Pallas kernels for 0%

commit v1 on v0

v1 whole, which is shorter than its diff:
```python
import functools

import jax
import jax.numpy as jnp
from jax import lax
from jax.experimental import pallas as pl
from jax.experimental.pallas import tpu as pltpu
from jax.sharding import PartitionSpec as P

MESH = pl.DeviceIdType.MESH
F32 = jnp.float32
BF16 = jnp.bfloat16

NX = 4
NY = 4
NZ = 8
NS = 4
HEAD = 128
TOK = 128
CACHE = 256
CQ = CACHE // NY
TQ = TOK // NY
KEYS = CQ + TQ
META = 2 * KEYS
ROWS = META + 16
FEAT = 512
SPAN = NY * FEAT
MASKED = -1e30
SCALE = HEAD ** (-0.5) * 1.4426950408889634


def nt(a, b):
    return lax.dot_general(a, b, (((1,), (1,)), ((), ())), preferred_element_type=F32)


def tn(a, b):
    return lax.dot_general(a, b, (((0,), (0,)), ((), ())), preferred_element_type=F32)


def pick(rows, wide, step, first):
    r = lax.broadcasted_iota(jnp.int32, (rows, wide), 0)
    c = lax.broadcasted_iota(jnp.int32, (rows, wide), 1)
    return jnp.where(c == step * r + first, 1.0, 0.0).astype(BF16)


def kernel(
    valid_ref, q_hbm, ik_hbm, iv_hbm, ck_hbm, cv_hbm, w_hbm, out_ref,
    q_raw, ck_raw, cv_raw, ik_raw, iv_raw,
    q_all, kv, bias, m_ref, l_ref, acc,
    o_send, o_recv, lse_send, lse_recv,
    att, wall, r_send, r_recv, own_out,
    local_sem, q_ss, q_rs, kv_ss, kv_rs, sib_ss, sib_rs, o_ss, o_rs, e_ss, e_rs,
    w_ss, w_rs, ws_ss, ws_rs, a_ss, a_rs, r_ss, r_rs,
):
    ctx = lax.axis_index("ctx")
    tp = lax.axis_index("tp")
    x, y = tp // NY, tp % NY
    z, shard = ctx // NS, ctx % NS
    y_hi, core = shard // 2, shard % 2
    quarter = y_hi * (NY - 1 - y) + (1 - y_hi) * y
    up = (lax.rem(z + 1, NZ) * NS + shard, tp)
    down = (lax.rem(z + NZ - 1, NZ) * NS + shard, tp)
    sibling = (z * NS + y_hi * 2 + (1 - core), tp)
    mirror = (z * NS + (1 - y_hi) * 2 + core, x * NY + (NY - 1 - y))
    y_at = [lax.rem(y + d, NY) for d in range(NY)]
    x_at = [lax.rem(x + d, NX) for d in range(NX)]
    y_peer = [(ctx, x * NY + y_at[d]) for d in range(NY)]
    x_peer = [(ctx, x_at[d] * NY + y) for d in range(NX)]

    def send(src, dst, ss, rs, to):
        copy = pltpu.make_async_remote_copy(
            src_ref=src, dst_ref=dst, send_sem=ss, recv_sem=rs, device_id=to, device_id_type=MESH
        )
        copy.start()
        return copy

    def fetch(src, dst, sem):
        copy = pltpu.make_async_copy(src, dst, sem)
        copy.start()
        return copy

    sent = []

    c_at = pl.multiple_of(quarter * (CQ * NX), CQ * NX)
    t_at = pl.multiple_of(quarter * (TQ * NX), TQ * NX)
    loads = [
        fetch(ck_hbm.at[pl.ds(c_at, CQ * NX)], ck_raw, local_sem.at[0]),
        fetch(ik_hbm.at[pl.ds(t_at, TQ * NX)], ik_raw, local_sem.at[1]),
        fetch(cv_hbm.at[pl.ds(c_at, CQ * NX)], cv_raw, local_sem.at[2]),
        fetch(iv_hbm.at[pl.ds(t_at, TQ * NX)], iv_raw, local_sem.at[3]),
        fetch(q_hbm, q_raw, local_sem.at[4]),
    ]

    barrier = pltpu.get_barrier_semaphore()
    partners = [up, down, sibling, mirror] + y_peer[1:] + x_peer[1:]
    for partner in partners:
        pl.semaphore_signal(barrier, inc=1, device_id=partner, device_id_type=MESH)

    take_c = pick(CQ, CQ * NX, NX, x)
    take_t = pick(TQ, TQ * NX, NX, x)
    own = kv.at[z, shard]
    own[META:ROWS] = jnp.full((16, HEAD), valid_ref[0].astype(F32), F32).astype(BF16)
    loads[0].wait()
    own[0:CQ] = jnp.dot(take_c, ck_raw[...], preferred_element_type=F32).astype(BF16)
    loads[1].wait()
    own[CQ:KEYS] = jnp.dot(take_t, ik_raw[...], preferred_element_type=F32).astype(BF16)
    loads[2].wait()
    own[KEYS:KEYS + CQ] = jnp.dot(take_c, cv_raw[...], preferred_element_type=F32).astype(BF16)
    loads[3].wait()
    own[KEYS + CQ:META] = jnp.dot(take_t, iv_raw[...], preferred_element_type=F32).astype(BF16)
    loads[4].wait()
    for h in range(2):
        q_all[y, h * TOK:(h + 1) * TOK] = jnp.dot(
            pick(TOK, 2 * TOK, 2, h), q_raw[...], preferred_element_type=F32
        ).astype(BF16)

    pl.semaphore_wait(barrier, len(partners))

    types = [shard, (1 - y_hi) * 2 + core]
    sib_types = [y_hi * 2 + (1 - core), (1 - y_hi) * 2 + (1 - core)]

    def slot(k):
        return lax.rem(z + k + NZ, NZ)

    def ring(way, kind, step):
        at = kv.at[slot(-step if way == 0 else step), types[kind]]
        sent.append(
            send(at, at, kv_ss.at[way, kind, step], kv_rs.at[way, kind, step], up if way == 0 else down)
        )

    def to_sibling(kind, k, index):
        at = kv.at[slot(k), types[kind]]
        sent.append(send(at, at, sib_ss.at[kind, index], sib_rs.at[kind, index], sibling))

    def arrived(ref, sem):
        pltpu.make_async_copy(ref, ref, sem).wait()

    mirrored = send(own, own, kv_ss.at[0, 0, 4], kv_rs.at[0, 0, 4], mirror)
    sent.append(mirrored)
    ring(0, 0, 0)
    ring(1, 0, 0)
    to_sibling(0, 0, 0)
    q_own = q_all.at[y]
    for d in (2, 1, 3):
        sent.append(send(q_own, q_own, q_ss.at[d], q_rs.at[d], y_peer[d]))

    half = pl.ds(pl.multiple_of(core * TOK, TOK), TOK)
    for d in (2, 1, 3):
        sent.append(
            send(
                w_hbm.at[half, pl.ds(pl.multiple_of(x_at[d] * SPAN, SPAN), SPAN)],
                wall.at[x, half],
                w_ss.at[d],
                w_rs.at[d],
                x_peer[d],
            )
        )
    w_own = fetch(
        w_hbm.at[:, pl.ds(pl.multiple_of(x * SPAN, SPAN), SPAN)], wall.at[x], local_sem.at[5]
    )

    token = lax.broadcasted_iota(jnp.int32, (TQ, HEAD), 1) + ctx * TOK
    new_at = lax.broadcasted_iota(jnp.int32, (TQ, HEAD), 0) + quarter * TQ
    slot_at = (lax.broadcasted_iota(jnp.int32, (CQ, HEAD), 0) + quarter * CQ).astype(F32)

    def absorb(zs, first):
        for s in range(NS):
            live = kv[zs, s, META:META + 1, :].astype(F32)
            bias[s * KEYS:s * KEYS + CQ] = jnp.where(slot_at < live, 0.0, MASKED)
            bias[s * KEYS + CQ:(s + 1) * KEYS] = jnp.where(
                new_at + (zs * NS + s) * TOK <= token, 0.0, MASKED
            )

        def step(j, carry):
            keys = jnp.concatenate([kv[zs, s, 0:KEYS] for s in range(NS)], axis=0)
            values = jnp.concatenate([kv[zs, s, KEYS:META] for s in range(NS)], axis=0)
            b = bias[...]
            scores = nt(keys, q_all[j]) * SCALE + jnp.concatenate([b, b], axis=1)
            top = jnp.max(scores, axis=0, keepdims=True)
            if first:
                weights = jnp.exp2(scores - top)
                m_ref[j] = top
                l_ref[j] = jnp.sum(weights, axis=0, keepdims=True)
                acc[j] = tn(values, weights.astype(BF16))
            else:
                old = m_ref[j]
                new = jnp.maximum(old, top)
                rescale = jnp.exp2(old - new)
                weights = jnp.exp2(scores - new)
                m_ref[j] = new
                l_ref[j] = l_ref[j] * rescale + jnp.sum(weights, axis=0, keepdims=True)
                acc[j] = acc[j] * rescale + tn(values, weights.astype(BF16))
            return carry

        lax.fori_loop(0, NY, step, 0)

    arrived(kv.at[z, types[1]], kv_rs.at[0, 0, 4])
    ring(0, 1, 0)
    ring(1, 1, 0)
    to_sibling(1, 0, 0)
    for d in (1, 2, 3):
        arrived(q_all.at[y_at[d]], q_rs.at[NY - d])
    for kind in range(2):
        arrived(kv.at[z, sib_types[kind]], sib_rs.at[kind, 0])
    absorb(z, True)

    for k in range(1, 4):
        for kind in range(2):
            arrived(kv.at[slot(-k), types[kind]], kv_rs.at[0, kind, k - 1])
            if k < 3 or kind == 0:
                ring(0, kind, k)
            to_sibling(kind, -k, 2 * k - 1)
            arrived(kv.at[slot(k), types[kind]], kv_rs.at[1, kind, k - 1])
            if k < 3 or kind == 1:
                ring(1, kind, k)
            to_sibling(kind, k, 2 * k)
        for kind in range(2):
            arrived(kv.at[slot(-k), sib_types[kind]], sib_rs.at[kind, 2 * k - 1])
        absorb(slot(-k), False)
        for kind in range(2):
            arrived(kv.at[slot(k), sib_types[kind]], sib_rs.at[kind, 2 * k])
        absorb(slot(k), False)
    for kind in range(2):
        arrived(kv.at[slot(4), types[kind]], kv_rs.at[kind, kind, 3])
        to_sibling(kind, 4, 7)
    for kind in range(2):
        arrived(kv.at[slot(4), sib_types[kind]], sib_rs.at[kind, 7])
    absorb(slot(4), False)

    for d in (2, 1, 3, 0):
        j = y_at[d]
        total = l_ref[j]
        o_send[d] = (acc[j] / total).astype(BF16)
        lse_send[d] = jnp.broadcast_to(m_ref[j] + jnp.log2(total), (8, 2 * TOK))
        if d:
            sent.append(send(o_send.at[d], o_recv.at[d], o_ss.at[d], o_rs.at[d], y_peer[d]))
            sent.append(send(lse_send.at[d], lse_recv.at[d], e_ss.at[d], e_rs.at[d], y_peer[d]))
    for d in (1, 2, 3):
        arrived(o_recv.at[d], o_rs.at[d])
        arrived(lse_recv.at[d], e_rs.at[d])
    lse = [lse_send[0][0:1]] + [lse_recv[d][0:1] for d in (1, 2, 3)]
    top = jnp.maximum(jnp.maximum(lse[0], lse[1]), jnp.maximum(lse[2], lse[3]))
    share = [jnp.exp2(e - top) for e in lse]
    whole = share[0] + share[1] + share[2] + share[3]
    mixed = o_send[0].astype(F32) * (share[0] / whole)
    for d in (1, 2, 3):
        mixed = mixed + o_recv[d].astype(F32) * (share[d] / whole)
    for h in range(2):
        att[x, :, h * HEAD:(h + 1) * HEAD] = mixed[:, h * TOK:(h + 1) * TOK].T.astype(BF16)
    a_own = att.at[x]
    for d in (2, 1, 3):
        sent.append(send(a_own, a_own, a_ss.at[d], a_rs.at[d], x_peer[d]))

    for d in (1, 2, 3):
        at = wall.at[x_at[d], half]
        arrived(at, w_rs.at[NX - d])
        sent.append(send(at, at, ws_ss.at[d], ws_rs.at[d], sibling))
    w_own.wait()
    other = pl.ds(pl.multiple_of((1 - core) * TOK, TOK), TOK)
    for d in (1, 2, 3):
        arrived(att.at[x_at[d]], a_rs.at[NX - d])
        arrived(wall.at[x_at[d], other], ws_rs.at[d])

    for d in (2, 1, 3, 0):
        cols = pl.ds(pl.multiple_of(y_at[d] * FEAT, FEAT), FEAT)
        part = jnp.dot(att[0], wall[0, :, cols], preferred_element_type=F32)
        for i in range(1, NX):
            part = part + jnp.dot(att[i], wall[i, :, cols], preferred_element_type=F32)
        if d:
            r_send[d] = part.astype(BF16)
            sent.append(send(r_send.at[d], r_recv.at[d], r_ss.at[d], r_rs.at[d], y_peer[d]))
        else:
            own_out[...] = part
    for d in (1, 2, 3):
        arrived(r_recv.at[d], r_rs.at[d])
    out_ref[...] = (
        own_out[...] + r_recv[1].astype(F32) + r_recv[2].astype(F32) + r_recv[3].astype(F32)
    ).astype(BF16)
    for copy in sent:
        copy.wait_send()


def local(
    queries, incoming_keys, incoming_values, cache_keys, stored_value_rows, cache_valid, out_weight
):
    flat = [
        a.reshape(a.shape[0] * a.shape[1], a.shape[2])
        for a in (queries, incoming_keys, incoming_values, cache_keys, stored_value_rows)
    ]
    hbm = pl.BlockSpec(memory_space=pltpu.HBM)
    vmem = pltpu.VMEM
    dma = pltpu.SemaphoreType.DMA
    return pl.pallas_call(
        kernel,
        name="attend_project",
        out_shape=jax.ShapeDtypeStruct((TOK, FEAT), BF16),
        in_specs=[pl.BlockSpec(memory_space=pltpu.SMEM)] + [hbm] * 6,
        out_specs=pl.BlockSpec(memory_space=pltpu.VMEM),
        scratch_shapes=[
            vmem((2 * TOK, HEAD), BF16),
            vmem((CQ * NX, HEAD), BF16),
            vmem((CQ * NX, HEAD), BF16),
            vmem((TQ * NX, HEAD), BF16),
            vmem((TQ * NX, HEAD), BF16),
            vmem((NY, 2 * TOK, HEAD), BF16),
            vmem((NZ, NS, ROWS, HEAD), BF16),
            vmem((NS * KEYS, HEAD), F32),
            vmem((NY, 1, 2 * TOK), F32),
            vmem((NY, 1, 2 * TOK), F32),
            vmem((NY, HEAD, 2 * TOK), F32),
            vmem((NY, HEAD, 2 * TOK), BF16),
            vmem((NY, HEAD, 2 * TOK), BF16),
            vmem((NY, 8, 2 * TOK), F32),
            vmem((NY, 8, 2 * TOK), F32),
            vmem((NX, TOK, 2 * HEAD), BF16),
            vmem((NX, 2 * HEAD, SPAN), BF16),
            vmem((NY, TOK, FEAT), BF16),
            vmem((NY, TOK, FEAT), BF16),
            vmem((TOK, FEAT), F32),
            dma((6,)),
            dma((4,)), dma((4,)),
            dma((2, 2, 5)), dma((2, 2, 5)),
            dma((2, 8)), dma((2, 8)),
            dma((4,)), dma((4,)),
            dma((4,)), dma((4,)),
            dma((4,)), dma((4,)),
            dma((4,)), dma((4,)),
            dma((4,)), dma((4,)),
            dma((4,)), dma((4,)),
        ],
        compiler_params=pltpu.CompilerParams(
            collective_id=0, has_side_effects=True, vmem_limit_bytes=40 * 2**20
        ),
        cost_estimate=pl.CostEstimate(
            flops=2_200_000_000, bytes_accessed=6_000_000, transcendentals=3_200_000
        ),
    )(cache_valid, *flat, out_weight)


def solution(mesh):
    placed = (
        P("ctx", "tp", None),
        P("ctx", None, None),
        P("ctx", None, None),
        P("ctx", None, None),
        P("ctx", None, None),
        P("ctx"),
        P("tp", None),
    )
    return jax.shard_map(
        local, mesh=mesh, in_specs=placed, out_specs=P("ctx", "tp"), check_vma=False
    )
```

time: 472 us -> 75.9 us (0.16)
  the two profiles are of different devices: /device:TPU:64 before, /device:TPU:1 now
where the time goes in v1:
time: 75.9 us; the launch traced here: 74.4 us
  Pallas kernels  66.4 us (87%)
  local copies, waits for them, and re-layouts  7.38 us (10%)
    pallas_call x1, Pallas kernels, local(): pl.pallas_call(kernel, name='attend_project', out_shape=jax.ShapeDtypeStr...  66.4 us
    unnamed x13, local copies, waits for them, and re-layouts  7.38 us

profile of v1, /device:TPU:1, one launch (start us, length us, event | category | flops | bytes accessed | tf_op | source)
XLA Modules:
  0.0 74.4 jit_solution(7436744923210655680)
XLA Ops:
  0.7 0.0 copy-start
  0.7 2.2 %copy-done = bf16[256,8192]{1,0:T(8,128)(2,1)S(1)} copy-done((bf16[256,8192]{1,0:T(8,128)(2,1)S(1)}, bf16[256,8192]{1,0:T(8,128)(2,1)}, u32[]{:S(2)}) %copy-start) | copy-done | bytes 4194328
  2.8 0.0 copy-start.1
  2.8 0.9 %copy-done.1 = bf16[256,4,128]{2,1,0:T(4,128)(2,1)S(1)} copy-done((bf16[256,4,128]{2,1,0:T(4,128)(2,1)S(1)}, bf16[256,4,128]{2,1,0:T(4,128)(2,1)}, u32[]{:S(2)}) %copy-start.1) | copy-done | bytes 262168
  3.8 0.0 copy-start.2
  3.8 0.9 %copy-done.2 = bf16[256,4,128]{2,1,0:T(4,128)(2,1)S(1)} copy-done((bf16[256,4,128]{2,1,0:T(4,128)(2,1)S(1)}, bf16[256,4,128]{2,1,0:T(4,128)(2,1)}, u32[]{:S(2)}) %copy-start.2) | copy-done | bytes 262168
  4.7 0.0 copy-start.3
  4.7 0.9 %copy-done.3 = bf16[128,4,128]{2,1,0:T(4,128)(2,1)S(1)} copy-done((bf16[128,4,128]{2,1,0:T(4,128)(2,1)S(1)}, bf16[128,4,128]{2,1,0:T(4,128)(2,1)}, u32[]{:S(2)}) %copy-start.3) | copy-done | bytes 131096
  5.6 0.0 copy-start.4
  5.6 0.9 %copy-done.4 = bf16[128,4,128]{2,1,0:T(4,128)(2,1)S(1)} copy-done((bf16[128,4,128]{2,1,0:T(4,128)(2,1)S(1)}, bf16[128,4,128]{2,1,0:T(4,128)(2,1)}, u32[]{:S(2)}) %copy-start.4) | copy-done | bytes 131096
  6.6 0.0 copy-start.5
  6.6 0.8 %copy-done.5 = bf16[128,2,128]{2,1,0:T(2,128)(2,1)S(1)} copy-done((bf16[128,2,128]{2,1,0:T(2,128)(2,1)S(1)}, bf16[128,2,128]{2,1,0:T(2,128)(2,1)}, u32[]{:S(2)}) %copy-start.5) | copy-done | bytes 65560
  7.4 66.4 %attend_project.1 = bf16[128,512]{1,0:T(8,128)(2,1)S(1)} custom-call(s32[1]{0:T(128)S(6)} %copy.9.valid_ref, bf16[256,128]{1,0:T(8,128)(2,1)S(1)} %bitcast.9, bf16[512,128]{1,0:T(8,128)(2,1)S(1)} %bitcast.7, bf16[512,128]{1,0:T(8,128)(2,1)S(1)} %bitcast.8, bf16[1024,128]{1,0:T(8,128)(2,1)S(1)} %bitcast.5, bf16[1024,128]{1,0:T(8,128)(2,1)S(1)} %bitcast.6, ...), custom_call_target="tpu_custom_call" | custom-call | flops 2200000000 | bytes 6000000 | tf_op jit(solution)/shard_map/attend_project/pallas_call | solution.py:293
  73.8 0.7 copy.10
Async XLA Ops:
  0.7 2.2 %copy-start = (bf16[256,8192]{1,0:T(8,128)(2,1)S(1)}, bf16[256,8192]{1,0:T(8,128)(2,1)}, u32[]{:S(2)}) copy-start(bf16[256,8192]{1,0:T(8,128)(2,1)} %w_hbm.1) | copy-start | bytes 12582916
  2.8 0.9 %copy-start.1 = (bf16[256,4,128]{2,1,0:T(4,128)(2,1)S(1)}, bf16[256,4,128]{2,1,0:T(4,128)(2,1)}, u32[]{:S(2)}) copy-start(bf16[256,4,128]{2,1,0:T(4,128)(2,1)} %param.10) | copy-start | bytes 786436
  3.8 0.9 %copy-start.2 = (bf16[256,4,128]{2,1,0:T(4,128)(2,1)S(1)}, bf16[256,4,128]{2,1,0:T(4,128)(2,1)}, u32[]{:S(2)}) copy-start(bf16[256,4,128]{2,1,0:T(4,128)(2,1)} %param.11) | copy-start | bytes 786436
  4.7 0.9 %copy-start.3 = (bf16[128,4,128]{2,1,0:T(4,128)(2,1)S(1)}, bf16[128,4,128]{2,1,0:T(4,128)(2,1)}, u32[]{:S(2)}) copy-start(bf16[128,4,128]{2,1,0:T(4,128)(2,1)} %param.8) | copy-start | bytes 393220
  5.6 0.9 %copy-start.4 = (bf16[128,4,128]{2,1,0:T(4,128)(2,1)S(1)}, bf16[128,4,128]{2,1,0:T(4,128)(2,1)}, u32[]{:S(2)}) copy-start(bf16[128,4,128]{2,1,0:T(4,128)(2,1)} %param.9) | copy-start | bytes 393220
  6.6 0.8 %copy-start.5 = (bf16[128,2,128]{2,1,0:T(2,128)(2,1)S(1)}, bf16[128,2,128]{2,1,0:T(2,128)(2,1)}, u32[]{:S(2)}) copy-start(bf16[128,2,128]{2,1,0:T(2,128)(2,1)} %param.7) | copy-start | bytes 196612

commit v2 on v1

v2 whole, which is shorter than its diff:
```python
import jax
import jax.numpy as jnp
from jax import lax
from jax.experimental import pallas as pl
from jax.experimental.pallas import tpu as pltpu
from jax.sharding import PartitionSpec as P

MESH = pl.DeviceIdType.MESH
F32 = jnp.float32
BF16 = jnp.bfloat16

NX = 4
NY = 4
NZ = 8
NS = 4
HEAD = 128
TOK = 128
HALF = TOK // 2
CACHE = 256
CQ = CACHE // NY
TQ = TOK // NY
KEYS = CQ + TQ
META = 2 * KEYS
ROWS = META + 16
FEAT = 512
SPAN = NY * FEAT
MASKED = -1e30
VMEM_LIMIT = 64 * 2**20
SCALE = HEAD ** (-0.5) * 1.4426950408889634


def nt(a, b):
    return lax.dot_general(a, b, (((1,), (1,)), ((), ())), preferred_element_type=F32)


def tn(a, b):
    return lax.dot_general(a, b, (((0,), (0,)), ((), ())), preferred_element_type=F32)


def pick(rows, wide, step, first):
    r = lax.broadcasted_iota(jnp.int32, (rows, wide), 0)
    c = lax.broadcasted_iota(jnp.int32, (rows, wide), 1)
    return jnp.where(c == step * r + first, 1.0, 0.0).astype(BF16)


def kernel(
    valid_ref, q_hbm, ik_hbm, iv_hbm, ck_hbm, cv_hbm, w_hbm, out_ref,
    q_raw, ck_raw, cv_raw, ik_raw, iv_raw,
    q_all, kv, bias, m_ref, l_ref, acc,
    o_send, o_recv,
    att, wall, r_send, r_recv, far_out, own_out,
    local_sem, q_ss, q_rs, kv_ss, kv_rs, sib_ss, sib_rs, o_ss, o_rs,
    w_ss, w_rs, ws_ss, ws_rs, a_ss, a_rs, r_ss, r_rs,
):
    ctx = lax.axis_index("ctx")
    tp = lax.axis_index("tp")
    x, y = tp // NY, tp % NY
    z, shard = ctx // NS, ctx % NS
    y_hi, core = shard // 2, shard % 2
    quarter = y_hi * (NY - 1 - y) + (1 - y_hi) * y
    up = (lax.rem(z + 1, NZ) * NS + shard, tp)
    down = (lax.rem(z + NZ - 1, NZ) * NS + shard, tp)
    sibling = (z * NS + y_hi * 2 + (1 - core), tp)
    mirror = (z * NS + (1 - y_hi) * 2 + core, x * NY + (NY - 1 - y))
    y_at = [lax.rem(y + d, NY) for d in range(NY)]
    x_at = [lax.rem(x + d, NX) for d in range(NX)]
    y_peer = [(ctx, x * NY + y_at[d]) for d in range(NY)]
    x_peer = [(ctx, x_at[d] * NY + y) for d in range(NX)]

    def send(src, dst, ss, rs, to):
        copy = pltpu.make_async_remote_copy(
            src_ref=src, dst_ref=dst, send_sem=ss, recv_sem=rs, device_id=to, device_id_type=MESH
        )
        copy.start()
        return copy

    def fetch(src, dst, sem):
        copy = pltpu.make_async_copy(src, dst, sem)
        copy.start()
        return copy

    sent = []

    barrier = pltpu.get_barrier_semaphore()
    partners = [up, down, sibling, mirror] + y_peer[1:] + x_peer[1:]
    for partner in partners:
        pl.semaphore_signal(barrier, inc=1, device_id=partner, device_id_type=MESH)

    c_at = pl.multiple_of(quarter * (CQ * NX), CQ * NX)
    t_at = pl.multiple_of(quarter * (TQ * NX), TQ * NX)
    loads = [
        fetch(ck_hbm.at[pl.ds(c_at, CQ * NX)], ck_raw, local_sem.at[0]),
        fetch(ik_hbm.at[pl.ds(t_at, TQ * NX)], ik_raw, local_sem.at[1]),
        fetch(cv_hbm.at[pl.ds(c_at, CQ * NX)], cv_raw, local_sem.at[2]),
        fetch(iv_hbm.at[pl.ds(t_at, TQ * NX)], iv_raw, local_sem.at[3]),
        fetch(q_hbm, q_raw, local_sem.at[4]),
    ]

    take_c = pick(CQ, CQ * NX, NX, x)
    take_t = pick(TQ, TQ * NX, NX, x)
    own = kv.at[z, shard]
    own[META:ROWS] = jnp.full((16, HEAD), valid_ref[0].astype(F32), F32).astype(BF16)
    loads[0].wait()
    own[0:CQ] = jnp.dot(take_c, ck_raw[...], preferred_element_type=F32).astype(BF16)
    loads[1].wait()
    own[CQ:KEYS] = jnp.dot(take_t, ik_raw[...], preferred_element_type=F32).astype(BF16)
    loads[2].wait()
    own[KEYS:KEYS + CQ] = jnp.dot(take_c, cv_raw[...], preferred_element_type=F32).astype(BF16)
    loads[3].wait()
    own[KEYS + CQ:META] = jnp.dot(take_t, iv_raw[...], preferred_element_type=F32).astype(BF16)
    loads[4].wait()
    for i in range(4):
        q_all[0, i * HALF:(i + 1) * HALF] = jnp.dot(
            pick(HALF, 2 * TOK, 2, (i // 2) * TOK + i % 2), q_raw[...], preferred_element_type=F32
        ).astype(BF16)

    pl.semaphore_wait(barrier, len(partners))

    types = [shard, (1 - y_hi) * 2 + core]
    sib_types = [y_hi * 2 + (1 - core), (1 - y_hi) * 2 + (1 - core)]

    def slot(k):
        return lax.rem(z + k + NZ, NZ)

    def arrived(ref, sem):
        pltpu.make_async_copy(ref, ref, sem).wait()

    def ring(way, kind, step):
        at = kv.at[slot(-step if way == 0 else step), types[kind]]
        sent.append(
            send(at, at, kv_ss.at[way, kind, step], kv_rs.at[way, kind, step], up if way == 0 else down)
        )

    def to_sibling(kind, k):
        at = kv.at[slot(k), types[kind]]
        i = k % NZ
        sent.append(send(at, at, sib_ss.at[kind, i], sib_rs.at[kind, i], sibling))

    def from_sibling(k):
        for kind in range(2):
            arrived(kv.at[slot(k), sib_types[kind]], sib_rs.at[kind, k % NZ])

    def pass_on(kind, k):
        if k < 4 or kind == 0:
            arrived(kv.at[slot(-k), types[kind]], kv_rs.at[0, kind, k - 1])
            if k < 3 or (k == 3 and kind == 0):
                ring(0, kind, k)
            to_sibling(kind, -k)
        if k < 4 or kind == 1:
            arrived(kv.at[slot(k), types[kind]], kv_rs.at[1, kind, k - 1])
            if k < 3 or (k == 3 and kind == 1):
                ring(1, kind, k)
            to_sibling(kind, k)

    sent.append(send(own, own, kv_ss.at[0, 0, 4], kv_rs.at[0, 0, 4], mirror))
    ring(0, 0, 0)
    ring(1, 0, 0)
    to_sibling(0, 0)
    for d in (2, 1, 3):
        sent.append(send(q_all.at[0], q_all.at[NY - d], q_ss.at[d], q_rs.at[NY - d], y_peer[d]))

    half = pl.ds(pl.multiple_of(core * TOK, TOK), TOK)
    for d in (2, 1, 3):
        sent.append(
            send(
                w_hbm.at[half, pl.ds(pl.multiple_of(x_at[d] * SPAN, SPAN), SPAN)],
                wall.at[x, half],
                w_ss.at[d],
                w_rs.at[d],
                x_peer[d],
            )
        )
    w_own = fetch(
        w_hbm.at[:, pl.ds(pl.multiple_of(x * SPAN, SPAN), SPAN)], wall.at[x], local_sem.at[5]
    )

    lane = lax.broadcasted_iota(jnp.int32, (TQ, 2 * TOK), 1)
    token = lane // TOK * HALF + lane % HALF + ctx * TOK
    new_at = lax.broadcasted_iota(jnp.int32, (TQ, 2 * TOK), 0) + quarter * TQ
    slot_at = (lax.broadcasted_iota(jnp.int32, (CQ, HEAD), 0) + quarter * CQ).astype(F32)

    def absorb(k, rows=range(NY), first=False, masks=True):
        zs = slot(k)
        if masks:
            for s in range(NS):
                live = kv[zs, s, META:META + 1, :].astype(F32)
                b = jnp.where(slot_at < live, 0.0, MASKED)
                bias[s * KEYS:s * KEYS + CQ] = jnp.concatenate([b, b], axis=1)
                bias[s * KEYS + CQ:(s + 1) * KEYS] = jnp.where(
                    new_at + (zs * NS + s) * TOK <= token, 0.0, MASKED
                )
        keys = jnp.concatenate([kv[zs, s, 0:KEYS] for s in range(NS)], axis=0)
        values = jnp.concatenate([kv[zs, s, KEYS:META] for s in range(NS)], axis=0)

        def scored(j):
            return nt(keys, q_all[j]) * SCALE + bias[...]

        ready = scored(rows[0])
        for j in rows:
            scores = ready
            if j != rows[-1]:
                ready = scored(j + 1)
            top = jnp.max(scores, axis=0, keepdims=True)
            if first:
                weights = jnp.exp2(scores - top)
                m_ref[j] = top
                l_ref[j] = jnp.sum(weights, axis=0, keepdims=True)
                acc[j] = tn(values, weights.astype(BF16))
            else:
                old = m_ref[j]
                new = jnp.maximum(old, top)
                rescale = jnp.exp2(old - new)
                weights = jnp.exp2(scores - new)
                m_ref[j] = new
                l_ref[j] = l_ref[j] * rescale + jnp.sum(weights, axis=0, keepdims=True)
                acc[j] = acc[j] * rescale + tn(values, weights.astype(BF16))

    arrived(kv.at[z, types[1]], kv_rs.at[0, 0, 4])
    ring(0, 1, 0)
    ring(1, 1, 0)
    to_sibling(1, 0)
    pass_on(0, 1)
    from_sibling(0)
    absorb(0, range(1), first=True)
    pass_on(1, 1)
    for d in (1, 2, 3):
        arrived(q_all.at[d], q_rs.at[d])
    absorb(0, range(1, NY), first=True, masks=False)
    for k in range(2, 4):
        pass_on(0, k)
        from_sibling(1 - k)
        absorb(1 - k)
        pass_on(1, k)
        from_sibling(k - 1)
        absorb(k - 1)
    pass_on(0, 4)
    from_sibling(-3)
    absorb(-3)
    pass_on(1, 4)
    from_sibling(3)
    absorb(3)
    from_sibling(4)
    absorb(4)

    def parts(e):
        row = lax.broadcasted_iota(jnp.int32, (16, TOK), 0)
        high = e.astype(BF16).astype(F32)
        middle = (e - high).astype(BF16).astype(F32)
        return jnp.where(row == 0, high, jnp.where(row == 1, middle, e - high - middle)).astype(BF16)

    own_lse = [None, None]
    for h in range(2):
        lanes = slice(h * TOK, (h + 1) * TOK)
        for d in (2, 1, 3, 0):
            total = l_ref[d, :, lanes]
            o_send[h, d, 0:HEAD] = (acc[d, :, lanes] / total).astype(BF16)
            e = m_ref[d, :, lanes] + jnp.log2(total)
            if d:
                o_send[h, d, HEAD:] = parts(e)
                sent.append(send(o_send.at[h, d], o_recv.at[h, d], o_ss.at[h, d], o_rs.at[h, d], y_peer[d]))
            else:
                own_lse[h] = e
    for d in (1, 2, 3):
        at = wall.at[x_at[d], half]
        arrived(at, w_rs.at[NX - d])
        sent.append(send(at, at, ws_ss.at[d], ws_rs.at[d], sibling))
    for h in range(2):
        lse = [own_lse[h]]
        for d in (1, 2, 3):
            arrived(o_recv.at[h, d], o_rs.at[h, d])
            e = o_recv[h, d, HEAD:].astype(F32)
            lse.append(e[0:1] + e[1:2] + e[2:3])
        top = jnp.maximum(jnp.maximum(lse[0], lse[1]), jnp.maximum(lse[2], lse[3]))
        share = [jnp.exp2(e - top) for e in lse]
        whole = share[0] + share[1] + share[2] + share[3]
        mixed = o_send[h, 0, 0:HEAD].astype(F32) * (share[0] / whole)
        for d in (1, 2, 3):
            mixed = mixed + o_recv[h, d, 0:HEAD].astype(F32) * (share[d] / whole)
        turned = mixed.T.astype(BF16)
        att[h, x, :, 0:HEAD] = turned[0:HALF]
        att[h, x, :, HEAD:2 * HEAD] = turned[HALF:TOK]
        a_own = att.at[h, x]
        for d in (2, 1, 3):
            sent.append(send(a_own, a_own, a_ss.at[h, d], a_rs.at[h, d], x_peer[d]))
    w_own.wait()
    other = pl.ds(pl.multiple_of((1 - core) * TOK, TOK), TOK)

    at_end = jnp.logical_or(y == 0, y == NY - 1)
    near = y + 1 - 2 * lax.rem(y, 2)
    middle = jnp.where(y < 2, 2, 1)
    far = jnp.where(y < 2, 3, 0)

    def y_chip(i):
        return (ctx, x * NY + i)

    def project(h, i):
        cols = pl.ds(pl.multiple_of(i * FEAT, FEAT), FEAT)
        part = jnp.dot(att[h, 0], wall[0, :, cols], preferred_element_type=F32)
        for n in range(1, NX):
            part = part + jnp.dot(att[h, n], wall[n, :, cols], preferred_element_type=F32)
        return part

    def reduced(h, i, slot_there, to):
        return send(r_send.at[h, i], r_recv.at[h, slot_there], r_ss.at[h, i], r_rs.at[h, slot_there], to)

    for h in range(2):
        for d in (1, 2, 3):
            arrived(att.at[h, x_at[d]], a_rs.at[h, NX - d])
            if h == 0:
                arrived(wall.at[x_at[d], other], ws_rs.at[d])
        far_out[h] = project(h, far)

        @pl.when(at_end)
        def _():
            r_send[h, 0] = far_out[h].astype(BF16)
            reduced(h, 0, 3, y_chip(near))

        r_send[h, 1] = project(h, middle).astype(BF16)
        sent.append(reduced(h, 1, jnp.where(at_end, 0, 2), y_chip(middle)))
        r_send[h, 2] = project(h, near).astype(BF16)
        sent.append(reduced(h, 2, 1, y_chip(near)))
    for h in range(2):
        rows = slice(h * HALF, (h + 1) * HALF)
        own_out[rows] = project(h, y)

        @pl.when(jnp.logical_not(at_end))
        def _():
            arrived(r_recv.at[h, 3], r_rs.at[h, 3])
            r_send[h, 0] = (far_out[h] + r_recv[h, 3].astype(F32)).astype(BF16)
            reduced(h, 0, 0, y_chip(far))

    for h in range(2):
        rows = slice(h * HALF, (h + 1) * HALF)
        arrived(r_send.at[h, 0], r_ss.at[h, 0])

        @pl.when(jnp.logical_not(at_end))
        def _():
            arrived(r_recv.at[h, 2], r_rs.at[h, 2])
            own_out[rows] = own_out[rows] + r_recv[h, 2].astype(F32)

        for i in range(2):
            arrived(r_recv.at[h, i], r_rs.at[h, i])
        out_ref[rows] = (
            own_out[rows] + r_recv[h, 0].astype(F32) + r_recv[h, 1].astype(F32)
        ).astype(BF16)
    for copy in sent:
        copy.wait_send()


def local(
    queries, incoming_keys, incoming_values, cache_keys, stored_value_rows, cache_valid, out_weight
):
    flat = [
        a.reshape(a.shape[0] * a.shape[1], a.shape[2])
        for a in (queries, incoming_keys, incoming_values, cache_keys, stored_value_rows)
    ]
    hbm = pl.BlockSpec(memory_space=pltpu.HBM)
    vmem = pltpu.VMEM
    dma = pltpu.SemaphoreType.DMA
    return pl.pallas_call(
        kernel,
        name="attend_project",
        out_shape=jax.ShapeDtypeStruct((TOK, FEAT), BF16),
        in_specs=[pl.BlockSpec(memory_space=pltpu.SMEM)] + [hbm] * 6,
        out_specs=pl.BlockSpec(memory_space=pltpu.VMEM),
        scratch_shapes=[
            vmem((2 * TOK, HEAD), BF16),
            vmem((CQ * NX, HEAD), BF16),
            vmem((CQ * NX, HEAD), BF16),
            vmem((TQ * NX, HEAD), BF16),
            vmem((TQ * NX, HEAD), BF16),
            vmem((NY, 2 * TOK, HEAD), BF16),
            vmem((NZ, NS, ROWS, HEAD), BF16),
            vmem((NS * KEYS, 2 * TOK), F32),
            vmem((NY, 1, 2 * TOK), F32),
            vmem((NY, 1, 2 * TOK), F32),
            vmem((NY, HEAD, 2 * TOK), F32),
            vmem((2, NY, HEAD + 16, TOK), BF16),
            vmem((2, NY, HEAD + 16, TOK), BF16),
            vmem((2, NX, HALF, 2 * HEAD), BF16),
            vmem((NX, 2 * HEAD, SPAN), BF16),
            vmem((2, NY - 1, HALF, FEAT), BF16),
            vmem((2, NY, HALF, FEAT), BF16),
            vmem((2, HALF, FEAT), F32),
            vmem((TOK, FEAT), F32),
            dma((6,)),
            dma((4,)), dma((4,)),
            dma((2, 2, 5)), dma((2, 2, 5)),
            dma((2, 8)), dma((2, 8)),
            dma((2, 4)), dma((2, 4)),
            dma((4,)), dma((4,)),
            dma((4,)), dma((4,)),
            dma((2, 4)), dma((2, 4)),
            dma((2, 3)), dma((2, 4)),
        ],
        compiler_params=pltpu.CompilerParams(
            collective_id=0, has_side_effects=True, vmem_limit_bytes=VMEM_LIMIT
        ),
        cost_estimate=pl.CostEstimate(
            flops=2_200_000_000, bytes_accessed=6_000_000, transcendentals=3_200_000
        ),
    )(cache_valid, *flat, out_weight)


def solution(mesh):
    placed = (
        P("ctx", "tp", None),
        P("ctx", None, None),
        P("ctx", None, None),
        P("ctx", None, None),
        P("ctx", None, None),
        P("ctx"),
        P("tp", None),
    )
    return jax.shard_map(
        local, mesh=mesh, in_specs=placed, out_specs=P("ctx", "tp"), check_vma=False
    )
```

time: 75.9 us -> 60.6 us (0.80); the launches traced: 74.4 us -> 60.4 us
  Pallas kernels: 66.4 us -> 58.2 us
  local copies, waits for them, and re-layouts: 7.38 us -> 1.57 us
    pallas_call x1, Pallas kernels: 66.4 us -> 58.2 us  [local(): pl.pallas_call(kernel, name='attend_project', out_shape=jax.ShapeDtypeStr...]
    unnamed x13 -> x1, local copies, waits for them, and re-layouts: 7.38 us -> 1.57 us
where the time goes in v2:
time: 60.6 us; the launch traced here: 60.4 us
  Pallas kernels  58.2 us (96%)
  local copies, waits for them, and re-layouts  1.57 us (3%)
  between operations  0.66 us (1%)
    pallas_call x1, Pallas kernels, local(): pl.pallas_call(kernel, name='attend_project', out_shape=jax.ShapeDtypeStr...  58.2 us
    unnamed x1, local copies, waits for them, and re-layouts  1.57 us

profile of v2, /device:TPU:1, one launch (start us, length us, event | category | flops | bytes accessed | tf_op | source)
XLA Modules:
  0.0 60.4 jit_solution(10973269673420180081)
XLA Ops:
  0.7 58.2 %attend_project.1 = bf16[128,512]{1,0:T(8,128)(2,1)} custom-call(s32[1]{0:T(128)S(6)} %copy.9.valid_ref, bf16[256,128]{1,0:T(8,128)(2,1)} %bitcast.9, bf16[512,128]{1,0:T(8,128)(2,1)} %bitcast.7, bf16[512,128]{1,0:T(8,128)(2,1)} %bitcast.8, bf16[1024,128]{1,0:T(8,128)(2,1)} %bitcast.5, bf16[1024,128]{1,0:T(8,128)(2,1)} %bitcast.6, bf16[256,8192]{1,0:T(8,128)(2,1)} %w_hbm.1), custom_call_target="tpu_custom_call" | custom-call | flops 2200000000 | bytes 6000000 | tf_op jit(solution)/shard_map/attend_project/pallas_call | solution.py:360
  58.9 1.6 %copy.10 = bf16[128,512]{1,0:T(8,128)(2,1)} copy(bf16[128,512]{1,0:T(8,128)(2,1)} %attend_project.1) | data formatting | bytes 262144

commit v3 on v2

--- a/solution.py
+++ b/solution.py
@@ -20,12 +20,12 @@
 CQ = CACHE // NY
 TQ = TOK // NY
 KEYS = CQ + TQ
-META = 2 * KEYS
-ROWS = META + 16
+ROWS = 2 * KEYS
+DEAD = 64.0
 FEAT = 512
 SPAN = NY * FEAT
 MASKED = -1e30
-VMEM_LIMIT = 64 * 2**20
+VMEM_LIMIT = 40 * 2**20
 SCALE = HEAD ** (-0.5) * 1.4426950408889634
 
 
@@ -58,8 +58,7 @@
     z, shard = ctx // NS, ctx % NS
     y_hi, core = shard // 2, shard % 2
     quarter = y_hi * (NY - 1 - y) + (1 - y_hi) * y
-    up = (lax.rem(z + 1, NZ) * NS + shard, tp)
-    down = (lax.rem(z + NZ - 1, NZ) * NS + shard, tp)
+    z_peer = {k: (lax.rem(z + k + NZ, NZ) * NS + shard, tp) for k in (-2, -1, 1, 2)}
     sibling = (z * NS + y_hi * 2 + (1 - core), tp)
     mirror = (z * NS + (1 - y_hi) * 2 + core, x * NY + (NY - 1 - y))
     y_at = [lax.rem(y + d, NY) for d in range(NY)]
@@ -82,7 +81,7 @@
     sent = []
 
     barrier = pltpu.get_barrier_semaphore()
-    partners = [up, down, sibling, mirror] + y_peer[1:] + x_peer[1:]
+    partners = list(z_peer.values()) + [sibling, mirror] + y_peer[1:] + x_peer[1:]
     for partner in partners:
         pl.semaphore_signal(barrier, inc=1, device_id=partner, device_id_type=MESH)
 
@@ -99,63 +98,63 @@
     take_c = pick(CQ, CQ * NX, NX, x)
     take_t = pick(TQ, TQ * NX, NX, x)
     own = kv.at[z, shard]
-    own[META:ROWS] = jnp.full((16, HEAD), valid_ref[0].astype(F32), F32).astype(BF16)
     loads[0].wait()
-    own[0:CQ] = jnp.dot(take_c, ck_raw[...], preferred_element_type=F32).astype(BF16)
+    slot_at = lax.broadcasted_iota(jnp.int32, (CQ, HEAD), 0) + quarter * CQ
+    own[0:CQ] = jnp.where(
+        slot_at < valid_ref[0], jnp.dot(take_c, ck_raw[...], preferred_element_type=F32), DEAD
+    ).astype(BF16)
     loads[1].wait()
     own[CQ:KEYS] = jnp.dot(take_t, ik_raw[...], preferred_element_type=F32).astype(BF16)
     loads[2].wait()
     own[KEYS:KEYS + CQ] = jnp.dot(take_c, cv_raw[...], preferred_element_type=F32).astype(BF16)
     loads[3].wait()
-    own[KEYS + CQ:META] = jnp.dot(take_t, iv_raw[...], preferred_element_type=F32).astype(BF16)
+    own[KEYS + CQ:ROWS] = jnp.dot(take_t, iv_raw[...], preferred_element_type=F32).astype(BF16)
+    pl.semaphore_wait(barrier, len(partners))
+
+    types = [shard, (1 - y_hi) * 2 + core]
+    sib_types = [y_hi * 2 + (1 - core), (1 - y_hi) * 2 + (1 - core)]
+
+    def slot(k):
+        return lax.rem(z + k + NZ, NZ)
+
+    def arrived(ref, sem):
+        pltpu.make_async_copy(ref, ref, sem).wait()
+
+    def ship(kind, k, hop):
+        at = kv.at[slot(k), types[kind]]
+        i = (k - hop) % NZ
+        sent.append(send(at, at, kv_ss.at[kind, i], kv_rs.at[kind, i], z_peer[hop]))
+
+    def spread(kind):
+        for hop in (2, -2, 1, -1):
+            ship(kind, 0, hop)
+
+    def to_sibling(kind, k):
+        at = kv.at[slot(k), types[kind]]
+        i = k % NZ
+        sent.append(send(at, at, sib_ss.at[kind, i], sib_rs.at[kind, i], sibling))
+
+    def from_sibling(k):
+        for kind in range(2):
+            arrived(kv.at[slot(k), sib_types[kind]], sib_rs.at[kind, k % NZ])
+
+    def take(kind, k):
+        arrived(kv.at[slot(k), types[kind]], kv_rs.at[kind, k % NZ])
+        if abs(k) == 2:
+            onward = 1 if k < 0 else -1
+            if k == (-2 if kind == 0 else 2):
+                ship(kind, k, 2 * onward)
+            ship(kind, k, onward)
+        to_sibling(kind, k)
+
+    sent.append(send(own, own, kv_ss.at[0, 0], kv_rs.at[0, 0], mirror))
+    spread(0)
+    to_sibling(0, 0)
     loads[4].wait()
     for i in range(4):
         q_all[0, i * HALF:(i + 1) * HALF] = jnp.dot(
             pick(HALF, 2 * TOK, 2, (i // 2) * TOK + i % 2), q_raw[...], preferred_element_type=F32
         ).astype(BF16)
-
-    pl.semaphore_wait(barrier, len(partners))
-
-    types = [shard, (1 - y_hi) * 2 + core]
-    sib_types = [y_hi * 2 + (1 - core), (1 - y_hi) * 2 + (1 - core)]
-
-    def slot(k):
-        return lax.rem(z + k + NZ, NZ)
-
-    def arrived(ref, sem):
-        pltpu.make_async_copy(ref, ref, sem).wait()
-
-    def ring(way, kind, step):
-        at = kv.at[slot(-step if way == 0 else step), types[kind]]
-        sent.append(
-            send(at, at, kv_ss.at[way, kind, step], kv_rs.at[way, kind, step], up if way == 0 else down)
-        )
-
-    def to_sibling(kind, k):
-        at = kv.at[slot(k), types[kind]]
-        i = k % NZ
-        sent.append(send(at, at, sib_ss.at[kind, i], sib_rs.at[kind, i], sibling))
-
-    def from_sibling(k):
-        for kind in range(2):
-            arrived(kv.at[slot(k), sib_types[kind]], sib_rs.at[kind, k % NZ])
-
-    def pass_on(kind, k):
-        if k < 4 or kind == 0:
-            arrived(kv.at[slot(-k), types[kind]], kv_rs.at[0, kind, k - 1])
-            if k < 3 or (k == 3 and kind == 0):
-                ring(0, kind, k)
-            to_sibling(kind, -k)
-        if k < 4 or kind == 1:
-            arrived(kv.at[slot(k), types[kind]], kv_rs.at[1, kind, k - 1])
-            if k < 3 or (k == 3 and kind == 1):
-                ring(1, kind, k)
-            to_sibling(kind, k)
-
-    sent.append(send(own, own, kv_ss.at[0, 0, 4], kv_rs.at[0, 0, 4], mirror))
-    ring(0, 0, 0)
-    ring(1, 0, 0)
-    to_sibling(0, 0)
     for d in (2, 1, 3):
         sent.append(send(q_all.at[0], q_all.at[NY - d], q_ss.at[d], q_rs.at[NY - d], y_peer[d]))
 
@@ -177,20 +176,18 @@
     lane = lax.broadcasted_iota(jnp.int32, (TQ, 2 * TOK), 1)
     token = lane // TOK * HALF + lane % HALF + ctx * TOK
     new_at = lax.broadcasted_iota(jnp.int32, (TQ, 2 * TOK), 0) + quarter * TQ
-    slot_at = (lax.broadcasted_iota(jnp.int32, (CQ, HEAD), 0) + quarter * CQ).astype(F32)
 
     def absorb(k, rows=range(NY), first=False, masks=True):
         zs = slot(k)
         if masks:
             for s in range(NS):
-                live = kv[zs, s, META:META + 1, :].astype(F32)
-                b = jnp.where(slot_at < live, 0.0, MASKED)
+                b = jnp.where(kv[zs, s, 0:CQ].astype(F32) == DEAD, MASKED, 0.0)
                 bias[s * KEYS:s * KEYS + CQ] = jnp.concatenate([b, b], axis=1)
                 bias[s * KEYS + CQ:(s + 1) * KEYS] = jnp.where(
                     new_at + (zs * NS + s) * TOK <= token, 0.0, MASKED
                 )
         keys = jnp.concatenate([kv[zs, s, 0:KEYS] for s in range(NS)], axis=0)
-        values = jnp.concatenate([kv[zs, s, KEYS:META] for s in range(NS)], axis=0)
+        values = jnp.concatenate([kv[zs, s, KEYS:ROWS] for s in range(NS)], axis=0)
 
         def scored(j):
             return nt(keys, q_all[j]) * SCALE + bias[...]
@@ -215,32 +212,39 @@
                 l_ref[j] = l_ref[j] * rescale + jnp.sum(weights, axis=0, keepdims=True)
                 acc[j] = acc[j] * rescale + tn(values, weights.astype(BF16))
 
-    arrived(kv.at[z, types[1]], kv_rs.at[0, 0, 4])
-    ring(0, 1, 0)
-    ring(1, 1, 0)
+    arrived(kv.at[z, types[1]], kv_rs.at[0, 0])
+    spread(1)
     to_sibling(1, 0)
-    pass_on(0, 1)
+    take(0, 2)
+    take(0, -2)
+    take(0, 1)
+    take(0, -1)
+    take(1, 2)
+    take(1, -2)
     from_sibling(0)
     absorb(0, range(1), first=True)
-    pass_on(1, 1)
+    take(1, 1)
+    take(1, -1)
     for d in (1, 2, 3):
         arrived(q_all.at[d], q_rs.at[d])
     absorb(0, range(1, NY), first=True, masks=False)
-    for k in range(2, 4):
-        pass_on(0, k)
-        from_sibling(1 - k)
-        absorb(1 - k)
-        pass_on(1, k)
-        from_sibling(k - 1)
-        absorb(k - 1)
-    pass_on(0, 4)
-    from_sibling(-3)
-    absorb(-3)
-    pass_on(1, 4)
-    from_sibling(3)
-    absorb(3)
-    from_sibling(4)
-    absorb(4)
+    from_sibling(2)
+    absorb(2)
+    take(0, 4)
+    from_sibling(-2)
+    absorb(-2)
+    take(0, 3)
+    take(0, -3)
+    from_sibling(1)
+    absorb(1)
+    take(1, 4)
+    from_sibling(-1)
+    absorb(-1)
+    take(1, 3)
+    take(1, -3)
+    for k in (4, 3, -3):
+        from_sibling(k)
+        absorb(k)
 
     def parts(e):
         row = lax.broadcasted_iota(jnp.int32, (16, TOK), 0)
@@ -385,7 +389,7 @@
             vmem((TOK, FEAT), F32),
             dma((6,)),
             dma((4,)), dma((4,)),
-            dma((2, 2, 5)), dma((2, 2, 5)),
+            dma((2, 8)), dma((2, 8)),
             dma((2, 8)), dma((2, 8)),
             dma((2, 4)), dma((2, 4)),
             dma((4,)), dma((4,)),
@@ -399,7 +403,7 @@
         cost_estimate=pl.CostEstimate(
             flops=2_200_000_000, bytes_accessed=6_000_000, transcendentals=3_200_000
         ),
-    )(cache_valid, *flat, out_weight)
+    )(cache_valid, *[pltpu.with_memory_space_constraint(a, pltpu.HBM) for a in flat + [out_weight]])
 
 
 def solution(mesh):

time: 60.6 us -> 57.2 us (0.944)
  Pallas kernels: 58.2 us -> 55.7 us
  local copies, waits for them, and re-layouts: 1.57 us -> 0.66 us
    pallas_call x1, Pallas kernels: 58.2 us -> 55.7 us  [local(): pl.pallas_call(kernel, name='attend_project', out_shape=jax.ShapeDtypeStr...]
    unnamed x1, local copies, waits for them, and re-layouts: 1.57 us -> 0.66 us
where the time goes in v3:
time: 57.2 us; the launch traced here: 57 us
  Pallas kernels  55.7 us (97%)
  local copies, waits for them, and re-layouts  0.66 us (1%)
  between operations  0.66 us (1%)
    pallas_call x1, Pallas kernels, local(): pl.pallas_call(kernel, name='attend_project', out_shape=jax.ShapeDtypeStr...  55.7 us

profile of v3, /device:TPU:1, one launch (start us, length us, event | category | flops | bytes accessed | tf_op | source)
XLA Modules:
  0.0 57.0 jit_solution(8095859065377201890)
XLA Ops:
  0.7 55.7 %attend_project.1 = bf16[128,512]{1,0:T(8,128)(2,1)S(1)} custom-call(s32[1]{0:T(128)S(6)} %copy.9.valid_ref, bf16[256,128]{1,0:T(8,128)(2,1)} %bitcast.9, bf16[512,128]{1,0:T(8,128)(2,1)} %bitcast.7, bf16[512,128]{1,0:T(8,128)(2,1)} %bitcast.8, bf16[1024,128]{1,0:T(8,128)(2,1)} %bitcast.5, bf16[1024,128]{1,0:T(8,128)(2,1)} %bitcast.6, bf16[256,8192]{1,0:T(8,128)(2,1)} %w_hbm.1), custom_call_target="tpu_custom_call" | custom-call | flops 2200000000 | bytes 6000000 | tf_op jit(solution)/shard_map/attend_project/pallas_call | solution.py:364
  56.4 0.7 %copy.10 = bf16[128,512]{1,0:T(8,128)(2,1)} copy(bf16[128,512]{1,0:T(8,128)(2,1)S(1)} %attend_project.1) | data formatting | bytes 262144

commit v4 on v3

--- a/solution.py
+++ b/solution.py
@@ -159,11 +159,16 @@
         sent.append(send(q_all.at[0], q_all.at[NY - d], q_ss.at[d], q_rs.at[NY - d], y_peer[d]))
 
     half = pl.ds(pl.multiple_of(core * TOK, TOK), TOK)
+    odd = lax.rem(z, 2)
+    mine = pl.ds(pl.multiple_of(core * TOK + odd * HALF, HALF), HALF)
+    theirs = pl.ds(pl.multiple_of(core * TOK + (1 - odd) * HALF, HALF), HALF)
+    z_pair = ((z + 1 - 2 * odd) * NS + shard, tp)
     for d in (2, 1, 3):
+        rows = mine if d == 2 else half
         sent.append(
             send(
-                w_hbm.at[half, pl.ds(pl.multiple_of(x_at[d] * SPAN, SPAN), SPAN)],
-                wall.at[x, half],
+                w_hbm.at[rows, pl.ds(pl.multiple_of(x_at[d] * SPAN, SPAN), SPAN)],
+                wall.at[x, rows],
                 w_ss.at[d],
                 w_rs.at[d],
                 x_peer[d],
@@ -228,20 +233,23 @@
     for d in (1, 2, 3):
         arrived(q_all.at[d], q_rs.at[d])
     absorb(0, range(1, NY), first=True, masks=False)
+    take(0, 4)
     from_sibling(2)
     absorb(2)
-    take(0, 4)
+    take(0, 3)
+    take(0, -3)
     from_sibling(-2)
     absorb(-2)
-    take(0, 3)
-    take(0, -3)
+    take(1, 4)
     from_sibling(1)
     absorb(1)
-    take(1, 4)
+    take(1, 3)
+    take(1, -3)
     from_sibling(-1)
     absorb(-1)
-    take(1, 3)
-    take(1, -3)
+    at = wall.at[x_at[2], mine]
+    arrived(at, w_rs.at[2])
+    sent.append(send(at, at, ws_ss.at[0], ws_rs.at[0], z_pair))
     for k in (4, 3, -3):
         from_sibling(k)
         absorb(k)
@@ -264,9 +272,12 @@
                 sent.append(send(o_send.at[h, d], o_recv.at[h, d], o_ss.at[h, d], o_rs.at[h, d], y_peer[d]))
             else:
                 own_lse[h] = e
-    for d in (1, 2, 3):
+    for d in (1, 3, 2):
         at = wall.at[x_at[d], half]
-        arrived(at, w_rs.at[NX - d])
+        if d == 2:
+            arrived(wall.at[x_at[d], theirs], ws_rs.at[0])
+        else:
+            arrived(at, w_rs.at[NX - d])
         sent.append(send(at, at, ws_ss.at[d], ws_rs.at[d], sibling))
     for h in range(2):
         lse = [own_lse[h]]

time: 57.2 us -> 54.8 us (0.958)
  the two profiles are of different devices: /device:TPU:1 before, /device:TPU:2 now
where the time goes in v4:
time: 54.8 us; the launch traced here: 54.7 us
  Pallas kernels  53.4 us (97%)
  local copies, waits for them, and re-layouts  0.66 us (1%)
  between operations  0.66 us (1%)
    pallas_call x1, Pallas kernels, local(): pl.pallas_call(kernel, name='attend_project', out_shape=jax.ShapeDtypeStr...  53.4 us

profile of v4, /device:TPU:2, one launch (start us, length us, event | category | flops | bytes accessed | tf_op | source)
XLA Modules:
  0.0 54.7 jit_solution(15884877018647792622)
XLA Ops:
  0.7 53.4 %attend_project.1 = bf16[128,512]{1,0:T(8,128)(2,1)S(1)} custom-call(s32[1]{0:T(128)S(6)} %copy.9.valid_ref, bf16[256,128]{1,0:T(8,128)(2,1)} %bitcast.9, bf16[512,128]{1,0:T(8,128)(2,1)} %bitcast.7, bf16[512,128]{1,0:T(8,128)(2,1)} %bitcast.8, bf16[1024,128]{1,0:T(8,128)(2,1)} %bitcast.5, bf16[1024,128]{1,0:T(8,128)(2,1)} %bitcast.6, bf16[256,8192]{1,0:T(8,128)(2,1)} %w_hbm.1), custom_call_target="tpu_custom_call" | custom-call | flops 2200000000 | bytes 6000000 | tf_op jit(solution)/shard_map/attend_project/pallas_call | solution.py:375
  54.0 0.7 %copy.10 = bf16[128,512]{1,0:T(8,128)(2,1)} copy(bf16[128,512]{1,0:T(8,128)(2,1)S(1)} %attend_project.1) | data formatting | bytes 262144
